TPU v7x, 32 devices: a whole 2x2x4 slice. The times are simulated.
32 devices in a mesh: groups: 2 (over y), dom: 4 (over z), ens: 2 (over x), rep: 2 (over core).
Axes of the slice: x: 2, y: 2, z: 4, core: 2. Of those that a mesh axis runs over, the one named last changes fastest.
Arguments:
- grid_h: float32 [4, 8192, 512], P(('groups', 'ens'), ('dom', 'rep')), parts along dimension 0, may hold values from -6 to 6
- mesh_h: float32 [4, 1024, 512], P(('groups', 'ens'), ('dom', 'rep')), parts along dimension 0, may hold values from -6 to 6
- cotangent: float32 [4, 1024, 512], P(('groups', 'ens'), ('dom', 'rep')), parts along dimension 0, may hold values from -6 to 6
- weights: float32 [6, 512, 512], replicated, may hold values from -0.25 to 0.25
- gains: float32 [2, 512], replicated, may hold values from 0.5 to 1.5
- g2m_send: int32 [8, 8, 16], P(('dom', 'rep')), may hold values from -1 to 1023, as said below
- m2m_send: int32 [8, 8, 16], P(('dom', 'rep')), may hold values from -1 to 127, as said below
- g2m_edges: int32 [2, 13312], P(None, ('dom', 'rep')), may hold values from -1 to 1151, as said below
- m2m_edges: int32 [2, 8192], P(None, ('dom', 'rep')), may hold values from -1 to 255, as said below
Outputs:
- grad_grid: float32 [4, 8192, 512], P(('groups', 'ens'), ('dom', 'rep')), parts along dimension 0
- grad_mesh: float32 [4, 1024, 512], P(('groups', 'ens'), ('dom', 'rep')), parts along dimension 0
- grad_weights: float32 [12, 512, 512], P('groups', ('dom', 'ens', 'rep')), parts along dimension 0
- grad_gains: float32 [4, 512], P('groups', ('dom', 'ens', 'rep')), parts along dimension 0
There are 2 independent parts, one for each index of `groups`. A program takes and returns all parts, laid end to end along the dimension named above; an argument that names none is the same for every part. Nothing has to cross between parts.
Inputs may be any that keep to these rules, and one draw needn't show every extreme that they name: `g2m_send`: send[q, b, k] is a row of band q or -1; band q fills the first slots of each row with its count, -1 after; a band sends nothing to itself; a band sends to a band not adjacent to it only in the first 2 slots; band 0 fills all 16 slots to band 1 and exactly 2 to band 8 - 1. Rows may repeat. `m2m_send`: as for g2m_send, with mesh rows. `g2m_edges`: row 0 holds senders, row 1 receivers (0 to 127, or -1). A sender at or above 1024 names a slot that the source band fills. Empty slots (receiver -1, sender 0) stand at the end of a band's slots; bands 0 and 7 have none. `m2m_edges`: as for g2m_edges, with 128 in place of 1024.
All inputs are finite; a program needn't handle non-finite values.
Results may differ from a plain program's by a relative error of at most 0.000082.
Values sent between devices are 32-bit elements; how exact they have to be, the bound alone decides.
A program may use at most 128 MiB of HBM per device.

v0:
```python
import jax
import jax.numpy as jnp
from jax import lax
from jax.sharding import PartitionSpec as P


def product(left, right):
    return jnp.dot(left, right, precision=lax.Precision.HIGHEST, preferred_element_type=jnp.float32)


def product_tn(left, right):
    return lax.dot_general(
        left,
        right,
        (((0,), (0,)), ((), ())),
        precision=lax.Precision.HIGHEST,
        preferred_element_type=jnp.float32,
    )


def product_nt(left, right):
    return lax.dot_general(
        left,
        right,
        (((1,), (1,)), ((), ())),
        precision=lax.Precision.HIGHEST,
        preferred_element_type=jnp.float32,
    )


def layer_norm(values, gain_row):
    centre_mean = jnp.mean(values, axis=-1, keepdims=True)
    centred = values - centre_mean
    variance = jnp.mean(centred * centred, axis=-1, keepdims=True)
    return centred * lax.rsqrt(variance + 1e-05) * gain_row


def pick_rows(values, send_rows):
    safe_rows = jnp.maximum(send_rows, 0).reshape(-1)
    picked = jnp.take(values, safe_rows, axis=0).reshape(send_rows.shape + (values.shape[1],))
    return jnp.where((send_rows >= 0)[..., None], picked, 0.0)


def return_rows(grad_rows, send_rows, local_rows):
    target_rows = jnp.where(send_rows >= 0, send_rows, local_rows).reshape(-1)
    flat_grads = grad_rows.reshape(-1, grad_rows.shape[-1])
    return jax.ops.segment_sum(flat_grads, target_rows, num_segments=local_rows + 1)[:local_rows]


def sender_index(edge_lists):
    senders = edge_lists[0]
    return senders


def fetch_table(proj, send_rows, graph_name):
    feature_width = proj.shape[1]
    outgoing = pick_rows(proj, send_rows)
    if graph_name == "grid":
        arrived = lax.all_to_all(outgoing, ("dom", "rep"), split_axis=0, concat_axis=0, tiled=True)
    else:
        arrived = lax.all_to_all(outgoing, ("dom", "rep"), split_axis=0, concat_axis=0, tiled=True)
    table = jnp.concatenate([proj, arrived.reshape(-1, feature_width)], axis=0)
    return table


def give_back(d_table, send_rows, local_rows, graph_name):
    feature_width = d_table.shape[1]
    halo_rows = send_rows.shape[1]
    own_rows = d_table[:local_rows]
    outgoing = d_table[local_rows:].reshape(send_rows.shape[0], halo_rows, feature_width)
    if graph_name == "grid":
        returned = lax.all_to_all(outgoing, ("dom", "rep"), split_axis=0, concat_axis=0, tiled=True)
    else:
        returned = lax.all_to_all(outgoing, ("dom", "rep"), split_axis=0, concat_axis=0, tiled=True)
    summed = own_rows + return_rows(returned, send_rows, local_rows)
    return summed


def edge_forward(table, target, w_recv, w_out, gain_row, senders, receivers):
    recv_proj = product(target, w_recv)
    safe_recv = jnp.maximum(receivers, 0)
    pre_act = jnp.take(table, senders, axis=0) + jnp.take(recv_proj, safe_recv, axis=0)
    hidden = jax.nn.silu(pre_act)
    message = product(hidden, w_out)
    node_ids = jnp.arange(target.shape[0], dtype=jnp.int32)[:, None]
    incidence = (receivers[None, :] == node_ids).astype(jnp.float32)
    gathered = product(incidence, message)
    normed, norm_back = jax.vjp(layer_norm, gathered, gain_row)
    saved_state = (
        pre_act,
        hidden,
        incidence,
        norm_back,
        safe_recv,
        receivers,
        senders,
        table.shape[0],
    )
    return (target + normed, saved_state)


def edge_backward(d_out, target, w_recv, w_out, saved_state):
    pre_act, hidden, incidence, norm_back, safe_recv, receivers, senders, table_rows = saved_state
    d_gathered, d_gain = norm_back(d_out)
    d_message = jnp.where((receivers >= 0)[:, None], jnp.take(d_gathered, safe_recv, axis=0), 0.0)
    d_w_out = product_tn(hidden, d_message)
    sigmoid_pre = jax.nn.sigmoid(pre_act)
    d_pre = product_nt(d_message, w_out) * sigmoid_pre * (1.0 + pre_act * (1.0 - sigmoid_pre))
    d_recv = product(incidence, d_pre)
    d_w_recv = product_tn(target, d_recv)
    d_target = d_out + product_nt(d_recv, w_recv)
    d_table = jax.ops.segment_sum(d_pre, senders, num_segments=table_rows)
    return (d_target, d_table, d_w_recv, d_w_out, d_gain)


def body(grid_h, mesh_h, cotangent, weights, gains, g2m_send, m2m_send, g2m_edges, m2m_edges):
    grid_rows = grid_h[0]
    mesh_rows = mesh_h[0]
    grid_send = g2m_send[0]
    mesh_send = m2m_send[0]
    grid_count = grid_rows.shape[0]
    mesh_count = mesh_rows.shape[0]
    grid_proj = product(grid_rows, weights[0])
    grid_table = fetch_table(grid_proj, grid_send, "grid")
    grid_senders = sender_index(g2m_edges)
    mesh_mid, grid_saved = edge_forward(
        grid_table, mesh_rows, weights[1], weights[2], gains[0], grid_senders, g2m_edges[1]
    )
    mesh_proj = product(mesh_mid, weights[3])
    mesh_table = fetch_table(mesh_proj, mesh_send, "mesh")
    mesh_senders = sender_index(m2m_edges)
    mesh_final, mesh_saved = edge_forward(
        mesh_table, mesh_mid, weights[4], weights[5], gains[1], mesh_senders, m2m_edges[1]
    )
    d_mid, d_mesh_table, d_w_pr, d_w_p2, d_gain_p = edge_backward(
        cotangent[0], mesh_mid, weights[4], weights[5], mesh_saved
    )
    d_mesh_proj = give_back(d_mesh_table, mesh_send, mesh_count, "mesh")
    d_w_ps = product_tn(mesh_mid, d_mesh_proj)
    d_mid = d_mid + product_nt(d_mesh_proj, weights[3])
    d_mesh, d_grid_table, d_w_gr, d_w_g2, d_gain_g = edge_backward(
        d_mid, mesh_rows, weights[1], weights[2], grid_saved
    )
    d_grid_proj = give_back(d_grid_table, grid_send, grid_count, "grid")
    d_w_gs = product_tn(grid_rows, d_grid_proj)
    d_grid = product_nt(d_grid_proj, weights[0])
    all_weights = jnp.stack([d_w_gs, d_w_gr, d_w_g2, d_w_ps, d_w_pr, d_w_p2])
    all_gains = jnp.stack([d_gain_g, d_gain_p])
    weight_grads, gain_grads = (
        lax.psum_scatter(all_weights, ("dom", "ens", "rep"), scatter_dimension=1, tiled=True),
        lax.psum_scatter(all_gains, ("dom", "ens", "rep"), scatter_dimension=1, tiled=True),
    )
    return (d_grid[None], d_mesh[None], weight_grads, gain_grads)


def solution(mesh):
    return jax.shard_map(
        body,
        mesh=mesh,
        in_specs=(
            P(("groups", "ens"), ("dom", "rep"), None),
            P(("groups", "ens"), ("dom", "rep"), None),
            P(("groups", "ens"), ("dom", "rep"), None),
            P(),
            P(),
            P(("dom", "rep"), None, None),
            P(("dom", "rep"), None, None),
            P(None, ("dom", "rep")),
            P(None, ("dom", "rep")),
        ),
        out_specs=(
            P(("groups", "ens"), ("dom", "rep"), None),
            P(("groups", "ens"), ("dom", "rep"), None),
            P("groups", ("dom", "ens", "rep"), None),
            P("groups", ("dom", "ens", "rep")),
        ),
        check_vma=False,
    )
```

profile of v0, /device:TPU:0, one launch (start us, length us, event | category | flops | bytes accessed | tf_op | source)
XLA Modules:
  0.0 349.0 jit_solution(16962181404702873902)
XLA Ops:
  7.2 0.9 squeeze.58
  8.1 0.7 compare_bitcast_fusion.1
  8.8 0.8 squeeze.62
  9.6 6.0 %fusion.4 = f32[1024,512]{1,0:T(8,128)} fusion(f32[1,1024,512]{2,1,0:T(8,128)S(1)} %copy-done, f32[6,512,512]{2,1,0:T(8,128)} %param.16), kind=kOutput, calls=%fused_computation.22 | convolution fusion | flops 3221225472 | bytes 5242880 | tf_op jit(solution)/shard_map/dot_general | solution.py:8
  15.6 2.5 gather_fusion
  18.1 0.8 select_select_fusion.17
  18.9 6.6 %all-to-all-start = ((f32[8,16,512]{2,1,0:T(8,128)}), f32[8,16,512]{2,1,0:T(8,128)S(1)}, u32[]{:S(2)}, u32[]{:S(2)}) async-start(f32[8,16,512]{2,1,0:T(8,128)} %select_select_fusion.17), calls=%async_computation | async-start | bytes 524288 | tf_op jit(solution)/shard_map/all_to_all | solution.py:59
  25.7 1.9 fusion.48
  27.7 5.6 %gather_fusion.4 = f32[1664,512]{1,0:T(8,128)} fusion(f32[128,512]{1,0:T(8,128)S(1)} %fusion.48, s32[2048]{0:T(1024)S(1)} %get-tuple-element.50), kind=kCustom, calls=%fused_computation.clone | custom fusion | bytes 6822400 | tf_op jit(solution)/shard_map/jit(_take)/gather | solution.py:82
  33.3 1.9 all-to-all-done
  35.2 3.3 pad_maximum_fusion
  38.5 8.1 %gather_fusion.1 = f32[1664,512]{1,0:T(8,128)} fusion(f32[1152,512]{1,0:T(8,128)} %pad_maximum_fusion, s32[2048]{0:T(1024)S(1)} %get-tuple-element.51), kind=kCustom, calls=%fused_computation.5 | custom fusion | bytes 6822400 | tf_op jit(solution)/shard_map/jit(_take)/gather | solution.py:82
  46.6 3.5 %select_add_fusion = f32[1664,512]{1,0:T(8,128)S(1)} fusion(f32[1664,512]{1,0:T(8,128)} %gather_fusion.4, f32[1664,512]{1,0:T(8,128)} %gather_fusion.1, pred[1664]{0:T(1024)(128)(4,1)S(1)} %get-tuple-element.29, pred[1664]{0:T(1024)(128)(4,1)S(1)} %get-tuple-element.49), kind=kLoop, calls=%fused_computation.13 | loop fusion | flops 2555904 | bytes 10226944 | tf_op jit(solution)/shard_map/add | solution.py:82
  50.1 8.3 %fusion.45 = f32[1664,512]{1,0:T(8,128)S(1)} fusion(f32[6,512,512]{2,1,0:T(8,128)} %param.16, f32[1664,512]{1,0:T(8,128)S(1)} %select_add_fusion), kind=kOutput, calls=%fused_computation.70 | convolution fusion | flops 5237899264 | bytes 7864320 | tf_op jit(solution)/shard_map/dot_general | solution.py:8
  58.4 1.5 fusion.116
  60.2 1.9 fusion.42
  62.2 0.8 gather_fusion.2
  62.9 0.8 select_select_fusion.16
  63.7 3.7 %all-to-all-start.1 = ((f32[8,16,512]{2,1,0:T(8,128)}), f32[8,16,512]{2,1,0:T(8,128)S(1)}, u32[]{:S(2)}, u32[]{:S(2)}) async-start(f32[8,16,512]{2,1,0:T(8,128)} %select_select_fusion.16), calls=%async_computation.1 | async-start | bytes 524288 | tf_op jit(solution)/shard_map/all_to_all | solution.py:61
  67.4 1.9 fusion.39
  69.4 4.9 %gather_fusion.5 = f32[1024,512]{1,0:T(8,128)} fusion(f32[128,512]{1,0:T(8,128)S(1)} %fusion.39, s32[1024]{0:T(1024)S(1)} %get-tuple-element.54), kind=kCustom, calls=%fused_computation.1.clone | custom fusion | bytes 4198400 | tf_op jit(solution)/shard_map/jit(_take)/gather | solution.py:82
  74.3 2.8 all-to-all-done.1
  77.1 0.7 copy-done.16
  77.8 1.0 pad_maximum_fusion.1
  78.8 4.9 %gather_fusion.3 = f32[1024,512]{1,0:T(8,128)} fusion(f32[256,512]{1,0:T(8,128)S(1)} %pad_maximum_fusion.1, s32[1024]{0:T(1024)S(1)} %get-tuple-element.55), kind=kCustom, calls=%fused_computation.7 | custom fusion | bytes 4198400 | tf_op jit(solution)/shard_map/jit(_take)/gather | solution.py:82
  83.7 2.5 select_add_fusion.1
  86.2 5.7 %fusion.36 = f32[1024,512]{1,0:T(8,128)S(1)} fusion(f32[6,512,512]{2,1,0:T(8,128)} %param.16, f32[1024,512]{1,0:T(8,128)S(1)} %select_add_fusion.1), kind=kOutput, calls=%fused_computation.61 | convolution fusion | flops 3223322624 | bytes 5242880 | tf_op jit(solution)/shard_map/dot_general | solution.py:8
  92.0 1.0 fusion.117
  93.4 0.2 fusion.113
  93.7 4.9 %gather_fusion.6 = f32[1024,512]{1,0:T(8,128)} fusion(f32[128,512]{1,0:T(8,128)S(1)} %broadcast_add_fusion.1, s32[1024]{0:T(1024)S(1)} %get-tuple-element.54), kind=kCustom, calls=%fused_computation.3.clone | custom fusion | bytes 4198400 | tf_op jit(solution)/shard_map/jit(_take)/gather | solution.py:105
  98.6 8.0 %add_multiply_fusion.1 = f32[1024,512]{1,0:T(8,128)} fusion(f32[1024,512]{1,0:T(8,128)} %copy-done.14, f32[1024,512]{1,0:T(8,128)} %gather_fusion.6, pred[1024]{0:T(1024)(128)(4,1)S(1)} %get-tuple-element.33, pred[1024]{0:T(1024)(128)(4,1)S(1)} %get-tuple-element.32, f32[6,512,512]{2,1,0:T(8,128)} %param.16), kind=kOutput, calls=%fused_computation.26 | convolution fusion | flops 3226468352 | bytes 7342080 | tf_op jit(solution)/shard_map/dot_general | solution.py:22
  106.6 7.8 %scatter_custom_fusion = f32[256,512]{1,0:T(8,128)S(1)} fusion(s32[1024]{0:T(1024)S(1)} %bitcast.160, f32[1024,512]{1,0:T(8,128)} %add_multiply_fusion.1, f32[]{:T(128)} %constant.79.clone.1), kind=kCustom, calls=%fused_computation.117 | custom fusion | flops 524288 | bytes 524800 | tf_op jit(solution)/shard_map/scatter-add | solution.py:112
  114.5 0.7 slice.95
  115.2 4.0 %all-to-all-start.2 = ((f32[8,16,512]{2,1,0:T(8,128)}), f32[8,16,512]{2,1,0:T(8,128)}, u32[]{:S(2)}, u32[]{:S(2)}) async-start(f32[8,16,512]{2,1,0:T(8,128)} %bitcast.145), calls=%async_computation.2 | async-start | bytes 524288 | tf_op jit(solution)/shard_map/all_to_all | solution.py:74
  119.2 2.5 fusion.78
  121.7 0.7 copy-done.8
  122.4 3.1 convolution_add_fusion.2
  125.5 3.5 all-to-all-done.2
  129.0 2.5 scatter_custom_fusion.1
  131.5 2.6 multiply_reduce_fusion
  134.3 0.5 copy-done.6
  134.9 5.8 %gather_fusion.7 = f32[1664,512]{1,0:T(8,128)} fusion(f32[128,512]{1,0:T(8,128)S(1)} %broadcast_add_fusion, s32[2048]{0:T(1024)S(1)} %get-tuple-element.50), kind=kCustom, calls=%fused_computation.2.clone | custom fusion | bytes 6822400 | tf_op jit(solution)/shard_map/jit(_take)/gather | solution.py:105
  140.7 10.5 %add_multiply_fusion = f32[1664,512]{1,0:T(8,128)} fusion(f32[1664,512]{1,0:T(8,128)} %copy-done.1, f32[1664,512]{1,0:T(8,128)} %gather_fusion.7, pred[1664]{0:T(1024)(128)(4,1)S(1)} %get-tuple-element.29, pred[1664]{0:T(1024)(128)(4,1)S(1)} %get-tuple-element.28, f32[6,512,512]{2,1,0:T(8,128)} %param.16), kind=kOutput, calls=%fused_computation.14 | convolution fusion | flops 5243011072 | bytes 11275520 | tf_op jit(solution)/shard_map/dot_general | solution.py:22
  151.1 14.7 %scatter_custom_fusion.2 = f32[1152,512]{1,0:T(8,128)} fusion(s32[1664]{0:T(1024)S(1)} %get-tuple-element.23, f32[1664,512]{1,0:T(8,128)} %add_multiply_fusion, f32[]{:T(128)} %constant.79.clone.1), kind=kCustom, calls=%fused_computation.52 | custom fusion | flops 851968 | bytes 2359808 | tf_op jit(solution)/shard_map/scatter-add | solution.py:112
  165.8 1.7 slice.98
  167.5 3.4 all-to-all-start.3
  171.0 0.9 copy.33
  171.9 3.3 fusion.74
  175.3 5.3 %all-to-all-done.3 = f32[8,16,512]{2,1,0:T(8,128)S(1)} async-done(((f32[8,16,512]{2,1,0:T(8,128)}), f32[8,16,512]{2,1,0:T(8,128)S(1)}, u32[]{:S(2)}, u32[]{:S(2)}) %all-to-all-start.3) | async-done | bytes 262176 | tf_op jit(solution)/shard_map/all_to_all | solution.py:72
  180.6 3.0 scatter_custom_fusion.3
  183.6 7.0 %fusion.25 = f32[6,512,512]{1,2,0:T(8,128)} fusion(f32[1,1024,512]{2,1,0:T(8,128)S(1)} %copy-done, f32[1025,512]{1,0:T(8,128)} %scatter_custom_fusion.3, f32[1152,512]{1,0:T(8,128)} %scatter_custom_fusion.2), kind=kOutput, calls=%fused_computation.49 | convolution fusion | flops 3221749760 | bytes 7340032 | tf_op jit(solution)/shard_map/dot_general | solution.py:12
  190.7 2.0 fusion.19
  192.7 8.1 %fusion.29 = f32[6,512,512]{1,2,0:T(8,128)} fusion(f32[6,512,512]{1,2,0:T(8,128)} %fusion.19, f32[1664,512]{1,0:T(8,128)S(1)} %copy-done.3, pred[1664]{0:T(1024)(128)(4,1)S(1)} %get-tuple-element.29, pred[1664]{0:T(1024)(128)(4,1)S(1)} %get-tuple-element.28, f32[1664,512]{1,0:T(8,128)S(1)} %copy-done.2), kind=kOutput, calls=%fused_computation.51 | convolution fusion | flops 5239603200 | bytes 7867648 | tf_op jit(solution)/shard_map/dot_general | solution.py:12
  200.8 2.3 fusion.18
  203.1 2.1 fusion.17
  205.2 5.2 %fusion.21 = f32[6,512,512]{1,2,0:T(8,128)} fusion(f32[6,512,512]{1,2,0:T(8,128)} %fusion.17, f32[1024,512]{1,0:T(8,128)S(1)} %copy-done.13, pred[1024]{0:T(1024)(128)(4,1)S(1)} %get-tuple-element.33, pred[1024]{0:T(1024)(128)(4,1)S(1)} %get-tuple-element.32, f32[1024,512]{1,0:T(8,128)S(1)} %copy-done.15), kind=kOutput, calls=%fused_computation.47 | convolution fusion | flops 3224371200 | bytes 5244928 | tf_op jit(solution)/shard_map/dot_general | solution.py:12
  210.4 9.7 %copy.27 = f32[6,512,512]{2,0,1:T(8,128)} copy(f32[6,512,512]{1,2,0:T(8,128)} %fusion.21) | data formatting | bytes 12582912 | tf_op jit(solution)/shard_map/stack | solution.py:147
  220.1 0.9 copy-done.7
  221.1 3.1 fusion.32
  224.2 7.8 %reduce-scatter.7.cloned.1.call-done = f32[32,2]{1,0:T(8,128)} async-done(((f32[512,2]{1,0:T(8,128)}), f32[32,2]{1,0:T(8,128)}) %reduce-scatter.7.cloned.1.call-update) | async-done | bytes 272
  232.0 1.4 copy.34
  233.3 7.3 %convolution_bitcast_fusion = f32[1,1024,512]{2,1,0:T(8,128)} fusion(f32[6,512,512]{2,1,0:T(8,128)} %param.16, f32[1025,512]{1,0:T(8,128)} %scatter_custom_fusion.3, f32[1152,512]{1,0:T(8,128)} %scatter_custom_fusion.2), kind=kOutput, calls=%fused_computation.39 | convolution fusion | flops 3221749760 | bytes 7340032 | tf_op jit(solution)/shard_map/dot_general | solution.py:22
  240.6 99.1 %reduce-scatter.5.cloned.1.call-done = f32[6,32,512]{2,0,1:T(8,128)} async-done(((f32[6,512,512]{2,0,1:T(8,128)}), f32[6,32,512]{2,0,1:T(8,128)}) %reduce-scatter.5.cloned.1.call-update) | async-done | bytes 393232 | tf_op jit(solution)/shard_map/reduce_scatter | solution.py:150
  339.7 2.0 copy.28
  (72 shorter events, 1.5 us)
Async XLA Ops:
  7.2 2.4 copy-start
  15.6 9.9 %copy-start.19 = (s32[1,8,16]{2,1,0:T(8,128)S(1)}, s32[1,8,16]{2,1,0:T(8,128)}, u32[]{:S(2)}) copy-start(s32[1,8,16]{2,1,0:T(8,128)} %param.19) | copy-start | bytes 1540
  15.6 10.0 %copy-start.18 = (s32[2,1024]{1,0:T(2,128)S(1)}, s32[2,1024]{1,0:T(2,128)}, u32[]{:S(2)}) copy-start(s32[2,1024]{1,0:T(2,128)} %param.21) | copy-start | bytes 24580
  15.6 10.0 %copy-start.17 = (s32[2,1664]{1,0:T(2,128)S(1)}, s32[2,1664]{1,0:T(2,128)}, u32[]{:S(2)}) copy-start(s32[2,1664]{1,0:T(2,128)} %param.20) | copy-start | bytes 39940
  15.6 10.1 %copy-start.20 = (f32[2,512]{1,0:T(2,128)S(1)}, f32[2,512]{1,0:T(2,128)}, u32[]{:S(2)}) copy-start(f32[2,512]{1,0:T(2,128)} %param.17) | copy-start | bytes 12292
  15.6 10.1 %copy-start.10 = (f32[1,128,512]{2,1,0:T(8,128)S(1)}, f32[1,128,512]{2,1,0:T(8,128)}, u32[]{:S(2)}) copy-start(f32[1,128,512]{2,1,0:T(8,128)} %param.14) | copy-start | bytes 786436
  18.9 16.3 %all-to-all-start = ((f32[8,16,512]{2,1,0:T(8,128)}), f32[8,16,512]{2,1,0:T(8,128)S(1)}, u32[]{:S(2)}, u32[]{:S(2)}) async-start(f32[8,16,512]{2,1,0:T(8,128)} %select_select_fusion.17), calls=%async_computation | async-start | bytes 524288 | tf_op jit(solution)/shard_map/all_to_all | solution.py:59
  50.1 8.3 %copy-start.1 = (f32[1664,512]{1,0:T(8,128)}, f32[1664,512]{1,0:T(8,128)S(1)}, u32[]{:S(2)}) copy-start(f32[1664,512]{1,0:T(8,128)S(1)} %select_add_fusion) | copy-start | bytes 10223620
  63.7 13.3 %all-to-all-start.1 = ((f32[8,16,512]{2,1,0:T(8,128)}), f32[8,16,512]{2,1,0:T(8,128)S(1)}, u32[]{:S(2)}, u32[]{:S(2)}) async-start(f32[8,16,512]{2,1,0:T(8,128)} %select_select_fusion.16), calls=%async_computation.1 | async-start | bytes 524288 | tf_op jit(solution)/shard_map/all_to_all | solution.py:61
  77.1 0.7 copy-start.16
  86.2 5.8 %copy-start.14 = (f32[1024,512]{1,0:T(8,128)}, f32[1024,512]{1,0:T(8,128)S(1)}, u32[]{:S(2)}) copy-start(f32[1024,512]{1,0:T(8,128)S(1)} %select_add_fusion.1) | copy-start | bytes 6291460
  92.0 1.2 copy-start.4
  106.6 15.8 %copy-start.5 = (f32[1,128,512]{2,1,0:T(8,128)S(1)}, f32[1,128,512]{2,1,0:T(8,128)}, u32[]{:S(2)}) copy-start(f32[1,128,512]{2,1,0:T(8,128)} %param.15) | copy-start | bytes 786436
  115.2 13.8 %all-to-all-start.2 = ((f32[8,16,512]{2,1,0:T(8,128)}), f32[8,16,512]{2,1,0:T(8,128)}, u32[]{:S(2)}, u32[]{:S(2)}) async-start(f32[8,16,512]{2,1,0:T(8,128)} %bitcast.145), calls=%async_computation.2 | async-start | bytes 524288 | tf_op jit(solution)/shard_map/all_to_all | solution.py:74
  121.7 0.7 copy-start.8
  134.1 0.7 copy-start.6
  167.5 13.1 %all-to-all-start.3 = ((f32[8,16,512]{2,1,0:T(8,128)}), f32[8,16,512]{2,1,0:T(8,128)S(1)}, u32[]{:S(2)}, u32[]{:S(2)}) async-start(f32[8,16,512]{2,1,0:T(8,128)} %bitcast.30), calls=%async_computation.3 | async-start | bytes 524288 | tf_op jit(solution)/shard_map/all_to_all | solution.py:72
  170.9 61.0 %reduce-scatter.7.cloned.1.call-start = ((), (), s32[]{:S(2)}) async-start(), calls=%async_computation.7 | async-start | bytes 278528
  171.9 167.9 %reduce-scatter.5.cloned.1.call-start = ((), (), s32[]{:S(2)}) async-start(), calls=%async_computation.6 | async-start | bytes 8912896 | tf_op jit(solution)/shard_map/reduce_scatter | solution.py:150
  183.6 7.1 %copy-start.11 = (f32[1,128,512]{2,1,0:T(8,128)S(1)}, f32[1,128,512]{2,1,0:T(8,128)}, u32[]{:S(2)}) copy-start(f32[1,128,512]{2,1,0:T(8,128)} %param.14) | copy-start | bytes 786436
  183.6 9.1 %copy-start.2 = (f32[1664,512]{1,0:T(8,128)S(1)}, f32[1664,512]{1,0:T(8,128)}, u32[]{:S(2)}) copy-start(f32[1664,512]{1,0:T(8,128)} %copy-done.1) | copy-start | bytes 10223620
  183.6 9.1 %copy-start.3 = (f32[1664,512]{1,0:T(8,128)S(1)}, f32[1664,512]{1,0:T(8,128)}, u32[]{:S(2)}) copy-start(f32[1664,512]{1,0:T(8,128)} %gather_fusion.7) | copy-start | bytes 10223620
  192.7 8.2 %copy-start.12 = (f32[129,512]{1,0:T(8,128)S(1)}, f32[129,512]{1,0:T(8,128)}, u32[]{:S(2)}) copy-start(f32[129,512]{1,0:T(8,128)} %scatter_custom_fusion.1) | copy-start | bytes 792580
  192.7 10.4 %copy-start.9 = (f32[128,512]{1,0:T(8,128)S(1)}, f32[128,512]{1,0:T(8,128)}, u32[]{:S(2)}) copy-start(f32[128,512]{1,0:T(8,128)} %copy-done.8) | copy-start | bytes 786436
  192.7 12.5 %copy-start.15 = (f32[1024,512]{1,0:T(8,128)S(1)}, f32[1024,512]{1,0:T(8,128)}, u32[]{:S(2)}) copy-start(f32[1024,512]{1,0:T(8,128)} %copy-done.14) | copy-start | bytes 6291460
  200.8 4.3 %copy-start.13 = (f32[1024,512]{1,0:T(8,128)S(1)}, f32[1024,512]{1,0:T(8,128)}, u32[]{:S(2)}) copy-start(f32[1024,512]{1,0:T(8,128)} %gather_fusion.6) | copy-start | bytes 6291460
  220.1 1.0 copy-start.7
Sparse Core Ops, SparseCore 0:
  175.3 56.6 reduce-scatter.6
  236.0 103.6 reduce-scatter.4
where the time goes:
time: 354 us; the launch traced here: 349 us
  waiting for transfers between devices  120 us (34%)
  matrix products  95.3 us (27%)
  local copies, waits for them, and re-layouts  58.3 us (16%)
  other arithmetic  42.2 us (12%)
  starting transfers between devices  17.8 us (5%)
  between operations  15 us (4%)
    reduce_scatter x1, waiting for transfers between devices, body(): lax.psum_scatter(all_weights, ('dom', 'ens', 'rep'), scatter_dimension=1,...  99.1 us
    dot_general x6, matrix products, product_nt(): lax.dot_general(left, right, (((1,), (1,)), ((), ())), precision=lax.Prec...  34.5 us
    dot_general x10, matrix products, product(): jnp.dot(left, right, precision=lax.Precision.HIGHEST, preferred_element_t...  34.1 us
    dot_general x6, matrix products, product_tn(): lax.dot_general(left, right, (((0,), (0,)), ((), ())), precision=lax.Prec...  26.7 us
    scatter-add x2, other arithmetic, edge_backward(): d_table = jax.ops.segment_sum(d_pre, senders, num_segments=table_rows)  22.6 us
    gather x2, local copies, waits for them, and re-layouts, edge_forward(): jnp.take(table, senders, axis=0) + jnp.take(recv_proj, safe_recv, axis=0)  13 us
    gather x2, local copies, waits for them, and re-layouts, edge_backward(): jnp.take(d_gathered, safe_recv, axis=0)  10.7 us
    gather x2, local copies, waits for them, and re-layouts, edge_forward(): jnp.take(recv_proj, safe_recv, axis=0)  10.5 us
  transfers between devices with their start and end apart: 6, of which 6 were waited for; matrix products, arithmetic and copies ran while one was open for 22% of the time, Pallas kernels for 0%

commit v1 on v0

v1 whole, which is shorter than its diff:
```python
import functools

import jax
import jax.numpy as jnp
from jax import lax
from jax.experimental import pallas as pl
from jax.experimental.pallas import tpu as pltpu
from jax.sharding import PartitionSpec as P

F32 = jnp.float32
BF16 = jnp.bfloat16
MESH = pl.DeviceIdType.MESH

GS, GR, G2, PS, PR, P2 = range(6)


def split(x):
    hi = x.astype(BF16)
    return hi, (x - hi.astype(F32)).astype(BF16)


def dot(a, b, ca, cb):
    return lax.dot_general(a, b, (((ca,), (cb,)), ((), ())), preferred_element_type=F32)


def dot3(a, b, ca=1, cb=0):
    return dot(a[0], b[0], ca, cb) + (dot(a[0], b[1], ca, cb) + dot(a[1], b[0], ca, cb))


def dot2(sel, b, ca=1, cb=0):
    return dot(sel, b[0], ca, cb) + dot(sel, b[1], ca, cb)


def ones(mask):
    return jnp.where(mask, 1.0, 0.0).astype(BF16)


def tile_of(n, largest, unit=128):
    return max(t for t in range(unit, largest + 1, unit) if n % t == 0)


def loop(n, tile, fn):
    if n == tile:
        fn(0)
        return

    def step(i, carry):
        fn(pl.multiple_of(i * tile, tile))
        return carry

    lax.fori_loop(0, n // tile, step, 0)


def norm_stats(agg):
    mean = jnp.mean(agg, axis=-1, keepdims=True)
    cen = agg - mean
    rstd = lax.rsqrt(jnp.mean(cen * cen, axis=-1, keepdims=True) + 1e-05)
    return cen * rstd, rstd


def norm_back(d_out, unit, rstd, gain):
    d_unit = d_out * gain
    m1 = jnp.mean(d_unit, axis=-1, keepdims=True)
    m2 = jnp.mean(d_unit * unit, axis=-1, keepdims=True)
    return rstd * (d_unit - m1 - unit * m2), jnp.sum(d_out * unit, axis=0, keepdims=True)


def kernel(
    cfg,
    grid_in, mesh_in, cot_in, w_in, gains_in, gsend_in, msend_in, gedge_in, medge_in,
    *refs,
):
    bands, nx, nz, fused = cfg["bands"], cfg["nx"], cfg["nz"], cfg["fused"]
    refs = list(refs)
    out_grid, out_mesh, out_w, out_gain = refs[:4]
    refs = refs[4:]
    take = lambda: refs.pop(0)
    grid_v, w_v, wh, wl, gh, gl = take(), take(), take(), take(), take(), take()
    th, tl, col_s, col_r, act_d, eh, el = (take() for _ in range(7))
    mcol_s, mcol_r, dtab = take(), take(), take()
    pick_g, pick_m = take(), take()
    send_buf, land = take(), take()
    load_sem, halo_ss, halo_rs, out_sem = take(), take(), take(), take()
    if fused:
        dw, r1, r2, r3, gain_mine, gain_land = (take() for _ in range(6))
        s1s, s1r, s2s, s2r, s3s, s3r, gss, gsr = (take() for _ in range(8))
    else:
        dw = out_w

    dom, ens, rep = lax.axis_index("dom"), lax.axis_index("ens"), lax.axis_index("rep")
    me = dom * 2 + rep
    ng, d = grid_v.shape
    nm = mesh_in.shape[1]
    ne_g, ne_m = gedge_in.shape[1], medge_in.shape[1]
    nh = bands * 16
    tg, tm = ng + nh, nm + nh
    flat = (dom * nx + ens) * 2 + rep
    n_all = nz * nx * 2

    def band_id(b):
        return {"dom": b // 2, "rep": lax.rem(b, 2)}

    def flat_id(f):
        return {"dom": f // (2 * nx), "ens": lax.rem(f // 2, nx), "rep": lax.rem(f, 2)}

    loads = [pltpu.make_async_copy(grid_in.at[0], grid_v, load_sem.at[6])]
    loads[0].start()
    w_loads = {}
    for w in (GS, GR, G2, PS, PR, P2):
        w_loads[w] = pltpu.make_async_copy(w_in.at[w], w_v.at[w], load_sem.at[w])
        w_loads[w].start()

    barrier = pltpu.get_barrier_semaphore()
    if fused:
        for o in range(1, n_all):
            pl.semaphore_signal(barrier, inc=1, device_id=flat_id(lax.rem(flat + o, n_all)), device_id_type=MESH)
    else:
        for o in range(1, bands):
            pl.semaphore_signal(barrier, inc=1, device_id=band_id(lax.rem(me + o, bands)), device_id_type=MESH)

    for ph in range(4):
        land[ph, me] = jnp.zeros((16, d), F32)
        for o in range(2, bands - 1):
            land[ph, lax.rem(me + bands - o, bands), 8:16] = jnp.zeros((8, d), F32)

    def pick_matrix(send, rows):
        s = send[0]
        wide = jnp.broadcast_to(s[:, None, :], (bands, 16, 16)).reshape(nh, 16)
        slot = lax.rem(lax.broadcasted_iota(jnp.int32, (nh, 16), 0), 16)
        lane = lax.broadcasted_iota(jnp.int32, (nh, 16), 1)
        col = jnp.sum(jnp.where(slot == lane, wide, 0).astype(F32), axis=1, keepdims=True)
        return ones(col.astype(jnp.int32) == lax.broadcasted_iota(jnp.int32, (nh, rows), 1))

    pick_g[...] = pick_matrix(gsend_in, ng)
    pick_m[...] = pick_matrix(msend_in, nm)

    def columns(edges, dst_s, dst_r, n):
        for i in range(n // 128):
            for row, dst in ((0, dst_s), (1, dst_r)):
                line = edges[row : row + 1, i * 128 : (i + 1) * 128]
                dst[i * 128 : (i + 1) * 128, :] = jnp.broadcast_to(line.astype(F32), (128, 128)).T.astype(jnp.int32)

    def exchange(ph):
        copies = []
        for o in range(1, bands):
            to = lax.rem(me + o, bands)
            rows = 16 if o in (1, bands - 1) else 8
            c = pltpu.make_async_remote_copy(
                src_ref=send_buf.at[ph, to, 0:rows],
                dst_ref=land.at[ph, me, 0:rows],
                send_sem=halo_ss.at[ph, o],
                recv_sem=halo_rs.at[ph, o],
                device_id=band_id(to),
                device_id_type=MESH,
            )
            c.start()
            copies.append(c)
        return copies

    sends = []

    def arrived(copies):
        for c in copies:
            c.wait_recv()
        sends.extend(copies)

    loads[0].wait()

    def split_grid(r):
        hi, lo = split(grid_v[pl.ds(r, 256), :])
        gh[pl.ds(r, 256), :] = hi
        gl[pl.ds(r, 256), :] = lo

    loop(ng, 256, split_grid)
    send_buf[0] = dot2(pick_g[...], (gh[0:ng, :], gl[0:ng, :])).reshape(bands, 16, d)
    pl.semaphore_wait(barrier, (n_all if fused else bands) - 1)
    halo = exchange(0)

    def load_w(w):
        w_loads[w].wait()
        hi, lo = split(w_v[w])
        wh[w] = hi
        wl[w] = lo

    def wt(w):
        return wh[w], wl[w]

    def put_table(r, value):
        hi, lo = split(value)
        n = value.shape[0]
        th[pl.ds(r, n), :] = hi
        tl[pl.ds(r, n), :] = lo

    load_w(GS)

    def project(r):
        put_table(r, dot3((gh[pl.ds(r, 256), :], gl[pl.ds(r, 256), :]), wt(GS)))

    loop(ng, 256, project)
    load_w(GR)
    mesh = mesh_in[0]
    mesh_s = split(mesh)
    put_table(tg, dot3(mesh_s, wt(GR)))
    columns(gedge_in, col_s, col_r, ne_g)
    columns(medge_in, mcol_s, mcol_r, ne_m)
    load_w(G2)
    load_w(PS)
    load_w(PR)
    load_w(P2)
    arrived(halo)
    hi, lo = split(land[0].reshape(nh, d))
    gh[ng:tg, :] = hi
    gl[ng:tg, :] = lo
    put_table(ng, dot3((hi, lo), wt(GS)))

    def gather(cs, cr, ne, table, tile, act):
        total = table + nm

        def step(r):
            s = cs[pl.ds(r, tile), :]
            t = cr[pl.ds(r, tile), :]
            lane = lax.broadcasted_iota(jnp.int32, (tile, 128), 1)
            parts = [ones(s == lane + j * 128) for j in range(table // 128)] + [ones(t == lane)]
            sel = jnp.concatenate(parts, axis=1)
            pre = dot2(sel, (th[0:total, :], tl[0:total, :]))
            sig = jax.nn.sigmoid(pre)
            hidden = pre * sig
            act[pl.ds(r, tile), :] = sig + hidden * (1.0 - sig)
            h, l = split(hidden)
            eh[pl.ds(r, tile), :] = h
            el[pl.ds(r, tile), :] = l

        loop(ne, tile, step)

    def incidence(edges, ne):
        return ones(edges[1:2, :] == lax.broadcasted_iota(jnp.int32, (nm, ne), 0))

    def back(cr, ne, tile, act, ds):
        def step(r):
            sel = ones(cr[pl.ds(r, tile), :] == lax.broadcasted_iota(jnp.int32, (tile, 128), 1))
            h, l = split(dot2(sel, ds) * act[pl.ds(r, tile), :])
            eh[pl.ds(r, tile), :] = h
            el[pl.ds(r, tile), :] = l

        loop(ne, tile, step)

    def scatter(edges, ne, first, n, tile):
        def step(r):
            node = lax.broadcasted_iota(jnp.int32, (tile, ne), 0) + (first + r)
            dtab[pl.ds(first + r, tile), :] = dot2(ones(edges[0:1, :] == node), (eh[0:ne, :], el[0:ne, :]))

        loop(n, tile, step)

    def store_dw(w, a, b):
        for t in range(4):
            cols = slice(t * 128, (t + 1) * 128)
            dw[w, t] = dot3((a[0][:, cols], a[1][:, cols]), b, 0, 0).reshape(dw.shape[2:])

    rs_pending = {}

    def rs1(w):
        if not fused:
            return
        c = pltpu.make_async_remote_copy(
            src_ref=dw.at[w, :, :, 1 - rep], dst_ref=r1.at[w], send_sem=s1s.at[w], recv_sem=s1r.at[w],
            device_id={"rep": 1 - rep}, device_id_type=MESH,
        )
        c.start()
        rs_pending[1, w] = [c]

    def rs2(w):
        if not fused:
            return
        arrived(rs_pending[1, w])
        r1[w] = r1[w] + dw[w, :, :, rep]
        rs_pending[2, w] = []
        for o in range(1, nx):
            to = lax.rem(ens + o, nx)
            c = pltpu.make_async_remote_copy(
                src_ref=r1.at[w, :, to], dst_ref=r2.at[w, o - 1], send_sem=s2s.at[w, o - 1], recv_sem=s2r.at[w, o - 1],
                device_id={"ens": to}, device_id_type=MESH,
            )
            c.start()
            rs_pending[2, w].append(c)

    def rs3(w):
        if not fused:
            return
        arrived(rs_pending[2, w])
        total = r1[w, :, ens]
        for o in range(nx - 1):
            total = total + r2[w, o]
        r2[w, 0] = total
        rs_pending[3, w] = []
        for o in range(1, nz):
            to = lax.rem(dom + o, nz)
            c = pltpu.make_async_remote_copy(
                src_ref=r2.at[w, 0, to], dst_ref=r3.at[w, o - 1], send_sem=s3s.at[w, o - 1], recv_sem=s3r.at[w, o - 1],
                device_id={"dom": to}, device_id_type=MESH,
            )
            c.start()
            rs_pending[3, w].append(c)

    def rs4(w):
        if not fused:
            return
        arrived(rs_pending[3, w])
        total = r2[w, 0, dom]
        for o in range(nz - 1):
            total = total + r3[w, o]
        out_w[w] = total

    tile_g = ne_g // 4 if (ne_g // 4) % 16 == 0 else 128
    tile_m = tile_of(ne_m, 512)
    gather(col_s, col_r, ne_g, tg, tile_g, act_d)
    sum_g = split(dot2(incidence(gedge_in, ne_g), (eh[0:ne_g, :], el[0:ne_g, :])))
    unit_g, rstd_g = norm_stats(dot3(sum_g, wt(G2)))
    mid = mesh + unit_g * gains_in[0:1, :]
    mid_s = split(mid)

    send_buf[1] = dot2(pick_m[...], mid_s).reshape(bands, 16, d)
    halo = exchange(1)
    put_table(0, dot3(mid_s, wt(PS)))
    put_table(tm, dot3(mid_s, wt(PR)))
    arrived(halo)
    halo_s = split(land[1].reshape(nh, d))
    put_table(nm, dot3(halo_s, wt(PS)))
    act_m = dtab
    gather(mcol_s, mcol_r, ne_m, tm, tile_m, act_m)
    sum_m = split(dot2(incidence(medge_in, ne_m), (eh[0:ne_m, :], el[0:ne_m, :])))
    unit_m, rstd_m = norm_stats(dot3(sum_m, wt(P2)))

    cot = cot_in[0]
    d_agg, d_gain_p = norm_back(cot, unit_m, rstd_m, gains_in[1:2, :])
    d_agg_s = split(d_agg)
    back(mcol_r, ne_m, tile_m, act_m, split(dot3(d_agg_s, wt(P2), 1, 1)))
    scatter(medge_in, ne_m, 0, tm, tile_of(tm, 384))
    send_buf[2] = dtab[nm:tm, :].reshape(bands, 16, d)
    halo = exchange(2)
    store_dw(P2, sum_m, d_agg_s)
    rs1(P2)
    d_recv_s = split(dot2(incidence(medge_in, ne_m), (eh[0:ne_m, :], el[0:ne_m, :])))
    store_dw(PR, mid_s, d_recv_s)
    rs1(PR)
    both = [jnp.concatenate([a, b], axis=0) for a, b in zip(mid_s, halo_s)]
    store_dw(PS, both, split(dtab[0:tm, :]))
    rs1(PS)
    d_mid = cot + dot3(d_recv_s, wt(PR), 1, 1)
    rs2(P2)
    arrived(halo)
    own = dtab[0:nm, :] + dot2(pick_m[...], split(land[2].reshape(nh, d)), 0, 0)
    d_mid = d_mid + dot3(split(own), wt(PS), 1, 1)

    d_agg, d_gain_g = norm_back(d_mid, unit_g, rstd_g, gains_in[0:1, :])
    if fused:
        row = lax.broadcasted_iota(jnp.int32, (8, d), 0)
        gain_mine[...] = jnp.where(row == 0, d_gain_g, jnp.where(row == 1, d_gain_p, 0.0))
        gain_copies = []
        for o in range(1, n_all):
            c = pltpu.make_async_remote_copy(
                src_ref=gain_mine, dst_ref=gain_land.at[o - 1], send_sem=gss.at[o - 1], recv_sem=gsr.at[o - 1],
                device_id=flat_id(lax.rem(flat + o, n_all)), device_id_type=MESH,
            )
            c.start()
            gain_copies.append(c)
    else:
        out_gain[0:1, :] = d_gain_g
        out_gain[1:2, :] = d_gain_p
    d_agg_s = split(d_agg)
    store_dw(G2, sum_g, d_agg_s)
    rs1(G2)
    rs2(PR)
    rs2(PS)
    back(col_r, ne_g, tile_g, act_d, split(dot3(d_agg_s, wt(G2), 1, 1)))
    d_recv_s = split(dot2(incidence(gedge_in, ne_g), (eh[0:ne_g, :], el[0:ne_g, :])))
    store_dw(GR, mesh_s, d_recv_s)
    rs1(GR)
    rs2(G2)
    rs3(P2)
    scatter(gedge_in, ne_g, ng, nh, 128)
    send_buf[3] = dtab[ng:tg, :].reshape(bands, 16, d)
    halo = exchange(3)
    rs2(GR)
    rs3(PR)
    scatter(gedge_in, ne_g, 0, ng, 256)
    rs3(PS)

    def split_dtab(r):
        hi, lo = split(dtab[pl.ds(r, 128), :])
        eh[pl.ds(r, 128), :] = hi
        el[pl.ds(r, 128), :] = lo

    loop(tg, 128, split_dtab)
    b = (eh[0:tg, :], el[0:tg, :])
    for t in range(4):
        cols = slice(t * 128, (t + 1) * 128)
        dw[GS, t] = dot3((gh[0:tg, cols], gl[0:tg, cols]), b, 0, 0).reshape(dw.shape[2:])
    rs1(GS)
    rs3(G2)
    out_mesh[0] = d_mid + dot3(d_recv_s, wt(GR), 1, 1)
    arrived(halo)
    ret = split(land[3].reshape(nh, d))

    def grid_step(r):
        own = dtab[pl.ds(r, 256), :] + dot2(pick_g[:, pl.ds(r, 256)], ret, 0, 0)
        grid_v[pl.ds(r, 256), :] = dot3(split(own), wt(GS), 1, 1)

    rs2(GS)
    rs3(GR)
    loop(ng, 256, grid_step)
    out_copy = pltpu.make_async_copy(grid_v, out_grid.at[0], out_sem)
    out_copy.start()
    rs3(GS)
    for w in (P2, PR, PS, G2, GR, GS):
        rs4(w)
    if fused:
        arrived(gain_copies)
        total = gain_mine[...]
        for o in range(n_all - 1):
            total = total + gain_land[o]
        width = d // n_all
        mine = jnp.zeros((8, width), F32)
        for j in range(n_all):
            mine = jnp.where(flat == j, total[:, j * width : (j + 1) * width], mine)
        out_gain[...] = mine[0:2]
    for c in sends:
        c.wait_send()
    out_copy.wait()


def body(cfg, grid_h, mesh_h, cotangent, weights, gains, g2m_send, m2m_send, g2m_edges, m2m_edges):
    bands, nx, nz, fused = cfg["bands"], cfg["nx"], cfg["nz"], cfg["fused"]
    ng, d = grid_h.shape[1:]
    nm = mesh_h.shape[1]
    ne_g, ne_m = g2m_edges.shape[1], m2m_edges.shape[1]
    nh = bands * 16
    tg, tm = ng + nh, nm + nh
    n_all = nz * nx * 2
    rows = d // n_all
    ne = max(ne_g, ne_m, tg)
    scratch = [
        pltpu.VMEM((ng, d), F32),
        pltpu.VMEM((6, d, d), F32),
        pltpu.VMEM((6, d, d), BF16),
        pltpu.VMEM((6, d, d), BF16),
        pltpu.VMEM((tg, d), BF16),
        pltpu.VMEM((tg, d), BF16),
        pltpu.VMEM((tg + nm, d), BF16),
        pltpu.VMEM((tg + nm, d), BF16),
        pltpu.VMEM((ne_g, 128), jnp.int32),
        pltpu.VMEM((ne_g, 128), jnp.int32),
        pltpu.VMEM((ne_g, d), F32),
        pltpu.VMEM((ne, d), BF16),
        pltpu.VMEM((ne, d), BF16),
        pltpu.VMEM((ne_m, 128), jnp.int32),
        pltpu.VMEM((ne_m, 128), jnp.int32),
        pltpu.VMEM((max(tg, ne_m), d), F32),
        pltpu.VMEM((nh, ng), BF16),
        pltpu.VMEM((nh, nm), BF16),
        pltpu.VMEM((4, bands, 16, d), F32),
        pltpu.VMEM((4, bands, 16, d), F32),
        pltpu.SemaphoreType.DMA((7,)),
        pltpu.SemaphoreType.DMA((4, bands)),
        pltpu.SemaphoreType.DMA((4, bands)),
        pltpu.SemaphoreType.DMA,
    ]
    if fused:
        scratch += [
            pltpu.VMEM((6, nz, nx, 2, rows, d), F32),
            pltpu.VMEM((6, nz, nx, rows, d), F32),
            pltpu.VMEM((6, nx - 1, nz, rows, d), F32),
            pltpu.VMEM((6, nz - 1, rows, d), F32),
            pltpu.VMEM((8, d), F32),
            pltpu.VMEM((n_all - 1, 8, d), F32),
            pltpu.SemaphoreType.DMA((6,)),
            pltpu.SemaphoreType.DMA((6,)),
            pltpu.SemaphoreType.DMA((6, nx - 1)),
            pltpu.SemaphoreType.DMA((6, nx - 1)),
            pltpu.SemaphoreType.DMA((6, nz - 1)),
            pltpu.SemaphoreType.DMA((6, nz - 1)),
            pltpu.SemaphoreType.DMA((n_all - 1,)),
            pltpu.SemaphoreType.DMA((n_all - 1,)),
        ]
        w_shape, gain_shape = (6, rows, d), (2, d // n_all)
    else:
        w_shape, gain_shape = (6, 4, d // 4, d), (2, d)
    vmem = pl.BlockSpec(memory_space=pltpu.VMEM)
    hbm = pl.BlockSpec(memory_space=pl.ANY)
    d_grid, d_mesh, d_w, d_gain = pl.pallas_call(
        functools.partial(kernel, cfg),
        out_shape=(
            jax.ShapeDtypeStruct((1, ng, d), F32),
            jax.ShapeDtypeStruct((1, nm, d), F32),
            jax.ShapeDtypeStruct(w_shape, F32),
            jax.ShapeDtypeStruct(gain_shape, F32),
        ),
        in_specs=[hbm, vmem, vmem, hbm, vmem, vmem, vmem, vmem, vmem],
        out_specs=(hbm, vmem, vmem, vmem),
        scratch_shapes=scratch,
        compiler_params=pltpu.CompilerParams(
            collective_id=0, has_side_effects=True, vmem_limit_bytes=62 * 1024 * 1024
        ),
    )(grid_h, mesh_h, cotangent, weights, gains, g2m_send, m2m_send, g2m_edges, m2m_edges)
    if not fused:
        axes = ("dom", "ens", "rep")
        d_w = lax.psum_scatter(d_w.reshape(6, d, d), axes, scatter_dimension=1, tiled=True)
        d_gain = lax.psum_scatter(d_gain, axes, scatter_dimension=1, tiled=True)
    return d_grid, d_mesh, d_w, d_gain


def solution(mesh):
    nz, nx, nr = mesh.shape["dom"], mesh.shape["ens"], mesh.shape["rep"]
    rows = 512 // (nz * nx * nr)
    cfg = dict(bands=nz * nr, nx=nx, nz=nz, fused=nz == 4 and nx > 1 and rows % 8 == 0)
    return jax.shard_map(
        functools.partial(body, cfg),
        mesh=mesh,
        in_specs=(
            P(("groups", "ens"), ("dom", "rep"), None),
            P(("groups", "ens"), ("dom", "rep"), None),
            P(("groups", "ens"), ("dom", "rep"), None),
            P(),
            P(),
            P(("dom", "rep"), None, None),
            P(("dom", "rep"), None, None),
            P(None, ("dom", "rep")),
            P(None, ("dom", "rep")),
        ),
        out_specs=(
            P(("groups", "ens"), ("dom", "rep"), None),
            P(("groups", "ens"), ("dom", "rep"), None),
            P("groups", ("dom", "ens", "rep"), None),
            P("groups", ("dom", "ens", "rep")),
        ),
        check_vma=False,
    )
```

time: 354 us -> 88.9 us (0.25); the launches traced: 349 us -> 88.7 us
  waiting for transfers between devices: 120 us -> 0 us
  matrix products: 95.3 us -> 0 us
  Pallas kernels: 0 us -> 82.9 us
  local copies, waits for them, and re-layouts: 58.3 us -> 5.16 us
  other arithmetic: 42.2 us -> 0 us
  starting transfers between devices: 17.8 us -> 0 us
  between operations: 15 us -> 0.67 us
    reduce_scatter x1 -> x0, waiting for transfers between devices: 99.1 us -> none  [body(): lax.psum_scatter(all_weights, ('dom', 'ens', 'rep'), scatter_dimension=1,...]
    dot_general x22 -> x0, matrix products: 95.3 us -> none  [the longest x6 34.5 us: product_nt(): lax.dot_general(left, right, (((1,), (1,)), ((), ())), precision=lax.Prec...]
    pallas_call x0 -> x1, Pallas kernels: none -> 82.9 us  [body(): pl.pallas_call(functools.partial(kernel, cfg), out_shape=(jax.ShapeDtypeS...]
    gather x8 -> x0, local copies, waits for them, and re-layouts: 37.4 us -> none  [the longest x2 13 us: edge_forward(): jnp.take(table, senders, axis=0) + jnp.take(recv_proj, safe_recv, axis=0)]
    scatter-add x4 -> x0, other arithmetic: 28.1 us -> none  [the longest x2 22.6 us: edge_backward(): d_table = jax.ops.segment_sum(d_pre, senders, num_segments=table_rows)]
    all_to_all x4 -> x0, starting transfers between devices: 17.7 us -> none  [the longest x2 10.2 us: fetch_table(): lax.all_to_all(outgoing, ('dom', 'rep'), split_axis=0, concat_axis=0, til...]
    all_to_all x4 -> x0, waiting for transfers between devices: 13.5 us -> none  [the longest x2 8.75 us: give_back(): lax.all_to_all(outgoing, ('dom', 'rep'), split_axis=0, concat_axis=0, til...]
    another operation x1 -> x0, local copies, waits for them, and re-layouts: 9.68 us -> none  [body(): all_weights = jnp.stack([d_w_gs, d_w_gr, d_w_g2, d_w_ps, d_w_pr, d_w_p2])]
  transfers between devices with their start and end apart: 6 -> 0, of which waited for: 6 -> 0; matrix products, arithmetic and copies ran while one was open for 22% -> 0% of each run, Pallas kernels for 0% -> 0%
where the time goes in v1:
time: 88.9 us; the launch traced here: 88.7 us
  Pallas kernels  82.9 us (93%)
  local copies, waits for them, and re-layouts  5.16 us (6%)
    pallas_call x1, Pallas kernels, body(): pl.pallas_call(functools.partial(kernel, cfg), out_shape=(jax.ShapeDtypeS...  82.9 us
    unnamed x10, local copies, waits for them, and re-layouts  5.16 us

profile of v1, /device:TPU:0, one launch (start us, length us, event | category | flops | bytes accessed | tf_op | source)
XLA Modules:
  0.0 88.7 jit_solution(3570696942866008547)
XLA Ops:
  0.6 82.9 %shard_map.120 = (f32[1,1024,512]{2,1,0:T(8,128)}, f32[1,128,512]{2,1,0:T(8,128)}, f32[6,32,512]{2,1,0:T(8,128)}, f32[2,32]{1,0:T(2,128)}) custom-call(f32[1,1024,512]{2,1,0:T(8,128)} %grid_in.1, f32[1,128,512]{2,1,0:T(8,128)} %mesh_in.1, f32[1,128,512]{2,1,0:T(8,128)} %cot_in.1, f32[6,512,512]{2,1,0:T(8,128)} %w_in.1, f32[2,512]{1,0:T(2,128)} %gains_in.1, ...), custom_call_target="tpu_custom_call" | custom-call | tf_op jit(solution)/shard_map/pallas_call | solution.py:489
  83.5 0.0 copy-start.1
  83.5 0.0 copy-start
  83.5 0.0 copy-start.2
  83.5 3.1 %copy.17 = f32[1,1024,512]{2,1,0:T(8,128)} copy(f32[1,1024,512]{2,1,0:T(8,128)} %get-tuple-element.8) | data formatting | bytes 4194304
  86.7 0.0 copy-done.1
  86.7 0.7 copy.18
  87.4 0.0 copy-done
  87.4 0.7 copy.19
  88.1 0.0 copy-done.2
  88.1 0.6 copy.20
Async XLA Ops:
  83.5 3.2 %copy-start.1 = (f32[1,128,512]{2,1,0:T(8,128)S(1)}, f32[1,128,512]{2,1,0:T(8,128)}, u32[]{:S(2)}) copy-start(f32[1,128,512]{2,1,0:T(8,128)} %get-tuple-element.9) | copy-start | bytes 786436
  83.5 3.9 %copy-start = (f32[6,32,512]{2,1,0:T(8,128)S(1)}, f32[6,32,512]{2,1,0:T(8,128)}, u32[]{:S(2)}) copy-start(f32[6,32,512]{2,1,0:T(8,128)} %get-tuple-element.10) | copy-start | bytes 1179652
  83.5 4.6 %copy-start.2 = (f32[2,32]{1,0:T(2,128)S(1)}, f32[2,32]{1,0:T(2,128)}, u32[]{:S(2)}) copy-start(f32[2,32]{1,0:T(2,128)} %get-tuple-element.11) | copy-start | bytes 772

commit v2 on v1

--- a/solution.py
+++ b/solution.py
@@ -12,6 +12,16 @@
 MESH = pl.DeviceIdType.MESH
 
 GS, GR, G2, PS, PR, P2 = range(6)
+
+UNITS = (
+    (P2, 0, 2, True),
+    (PR, 0, 2, False),
+    (PS, 0, 2, False),
+    (G2, 0, 2, False),
+    (GR, 0, 2, False),
+    (GS, 0, 1, False),
+    (GS, 1, 2, True),
+)
 
 
 def split(x):
@@ -79,11 +89,11 @@
     th, tl, col_s, col_r, act_d, eh, el = (take() for _ in range(7))
     mcol_s, mcol_r, dtab = take(), take(), take()
     pick_g, pick_m = take(), take()
-    send_buf, land = take(), take()
+    send_buf, land, far_send, far_land = take(), take(), take(), take()
     load_sem, halo_ss, halo_rs, out_sem = take(), take(), take(), take()
     if fused:
-        dw, r1, r2, r3, gain_mine, gain_land = (take() for _ in range(6))
-        s1s, s1r, s2s, s2r, s3s, s3r, gss, gsr = (take() for _ in range(8))
+        dw, r1, r2, r3, r4, gain_mine, gain_land = (take() for _ in range(7))
+        rs_ss, rs_rs, gss, gsr = (take() for _ in range(4))
     else:
         dw = out_w
 
@@ -119,9 +129,8 @@
             pl.semaphore_signal(barrier, inc=1, device_id=band_id(lax.rem(me + o, bands)), device_id_type=MESH)
 
     for ph in range(4):
-        land[ph, me] = jnp.zeros((16, d), F32)
-        for o in range(2, bands - 1):
-            land[ph, lax.rem(me + bands - o, bands), 8:16] = jnp.zeros((8, d), F32)
+        for o in [0] + list(range(2, bands - 1)):
+            land[ph, lax.rem(me + bands - o, bands)] = jnp.zeros((16, d), F32)
 
     def pick_matrix(send, rows):
         s = send[0]
@@ -140,14 +149,26 @@
                 line = edges[row : row + 1, i * 128 : (i + 1) * 128]
                 dst[i * 128 : (i + 1) * 128, :] = jnp.broadcast_to(line.astype(F32), (128, 128)).T.astype(jnp.int32)
 
+    quarter = d // 4
+    near = [o for o in (1, bands - 1)]
+    far = list(range(2, bands - 1))
+
     def exchange(ph):
         copies = []
-        for o in range(1, bands):
+        for o in near + far:
             to = lax.rem(me + o, bands)
-            rows = 16 if o in (1, bands - 1) else 8
+            if o in near:
+                src, dst = send_buf.at[ph, to], land.at[ph, me]
+            else:
+                for k in range(2):
+                    for c in range(4):
+                        far_send[ph, to, 4 * k + c : 4 * k + c + 1, :] = send_buf[
+                            ph, to, k : k + 1, c * quarter : (c + 1) * quarter
+                        ]
+                src, dst = far_send.at[ph, to], far_land.at[ph, me]
             c = pltpu.make_async_remote_copy(
-                src_ref=send_buf.at[ph, to, 0:rows],
-                dst_ref=land.at[ph, me, 0:rows],
+                src_ref=src,
+                dst_ref=dst,
                 send_sem=halo_ss.at[ph, o],
                 recv_sem=halo_rs.at[ph, o],
                 device_id=band_id(to),
@@ -163,6 +184,17 @@
         for c in copies:
             c.wait_recv()
         sends.extend(copies)
+
+    def halo_arrived(ph, copies):
+        arrived(copies)
+        for o in far:
+            src = lax.rem(me + bands - o, bands)
+            for k in range(2):
+                for c in range(4):
+                    land[ph, src, k : k + 1, c * quarter : (c + 1) * quarter] = far_land[
+                        ph, src, 4 * k + c : 4 * k + c + 1, :
+                    ]
+        return land[ph].reshape(nh, d)
 
     loads[0].wait()
 
@@ -207,8 +239,7 @@
     load_w(PS)
     load_w(PR)
     load_w(P2)
-    arrived(halo)
-    hi, lo = split(land[0].reshape(nh, d))
+    hi, lo = split(halo_arrived(0, halo))
     gh[ng:tg, :] = hi
     gl[ng:tg, :] = lo
     put_table(ng, dot3((hi, lo), wt(GS)))
@@ -251,64 +282,73 @@
 
         loop(n, tile, step)
 
+    def put_dw(w, t, value):
+        if not fused:
+            dw[w, t] = value
+            return
+        n = dw.shape[4]
+        for x in range(2):
+            for c in range(2):
+                dw[w, c, t, x] = value[(2 * x + c) * n : (2 * x + c + 1) * n]
+
     def store_dw(w, a, b):
         for t in range(4):
             cols = slice(t * 128, (t + 1) * 128)
-            dw[w, t] = dot3((a[0][:, cols], a[1][:, cols]), b, 0, 0).reshape(dw.shape[2:])
-
-    rs_pending = {}
-
-    def rs1(w):
+            put_dw(w, t, dot3((a[0][:, cols], a[1][:, cols]), b, 0, 0))
+
+    z_hi, z_lo = dom // 2, lax.rem(dom, 2)
+    rs_copies = {}
+
+    def rs_start(u, stage, pairs, device_id):
+        rs_copies[u] = []
+        for i, (src, dst) in enumerate(pairs):
+            c = pltpu.make_async_remote_copy(
+                src_ref=src, dst_ref=dst, send_sem=rs_ss.at[u, stage, i], recv_sem=rs_rs.at[u, stage, i],
+                device_id=device_id, device_id_type=MESH,
+            )
+            c.start()
+            rs_copies[u].append(c)
+
+    def rs(u, stage):
         if not fused:
             return
-        c = pltpu.make_async_remote_copy(
-            src_ref=dw.at[w, :, :, 1 - rep], dst_ref=r1.at[w], send_sem=s1s.at[w], recv_sem=s1r.at[w],
-            device_id={"rep": 1 - rep}, device_id_type=MESH,
-        )
-        c.start()
-        rs_pending[1, w] = [c]
-
-    def rs2(w):
-        if not fused:
-            return
-        arrived(rs_pending[1, w])
-        r1[w] = r1[w] + dw[w, :, :, rep]
-        rs_pending[2, w] = []
-        for o in range(1, nx):
-            to = lax.rem(ens + o, nx)
-            c = pltpu.make_async_remote_copy(
-                src_ref=r1.at[w, :, to], dst_ref=r2.at[w, o - 1], send_sem=s2s.at[w, o - 1], recv_sem=s2r.at[w, o - 1],
-                device_id={"ens": to}, device_id_type=MESH,
-            )
-            c.start()
-            rs_pending[2, w].append(c)
-
-    def rs3(w):
-        if not fused:
-            return
-        arrived(rs_pending[2, w])
-        total = r1[w, :, ens]
-        for o in range(nx - 1):
-            total = total + r2[w, o]
-        r2[w, 0] = total
-        rs_pending[3, w] = []
-        for o in range(1, nz):
-            to = lax.rem(dom + o, nz)
-            c = pltpu.make_async_remote_copy(
-                src_ref=r2.at[w, 0, to], dst_ref=r3.at[w, o - 1], send_sem=s3s.at[w, o - 1], recv_sem=s3r.at[w, o - 1],
-                device_id={"dom": to}, device_id_type=MESH,
-            )
-            c.start()
-            rs_pending[3, w].append(c)
-
-    def rs4(w):
-        if not fused:
-            return
-        arrived(rs_pending[3, w])
-        total = r2[w, 0, dom]
-        for o in range(nz - 1):
-            total = total + r3[w, o]
-        out_w[w] = total
+        w, lo, hi, z_first = UNITS[u]
+        half = out_w.shape[1] // 2
+        rows = slice(lo * half, hi * half)
+        if stage > 0:
+            arrived(rs_copies[u])
+        to_x = {"ens": 1 - ens}
+        to_z = {"dom": 2 * z_hi + (1 - z_lo)}
+        to_far = {"dom": 2 * (1 - z_hi) + z_lo}
+        if stage == 0:
+            rs_start(u, 0, [(dw.at[w, 1 - rep, :, :, rows], r1.at[w, :, :, rows])], {"rep": 1 - rep})
+        elif stage == 1:
+            r1[w, :, :, rows] = r1[w, :, :, rows] + dw[w, rep, :, :, rows]
+            if z_first:
+                pairs = [(r1.at[w, 2 * p + 1 - z_lo, :, rows], r2.at[w, 2 * p : 2 * p + 2, rows]) for p in range(2)]
+                rs_start(u, 1, pairs, to_z)
+            else:
+                rs_start(u, 1, [(r1.at[w, :, 1 - ens, rows], r2.at[w, :, rows])], to_x)
+        elif stage == 2:
+            if z_first:
+                for p in range(2):
+                    both = slice(2 * p, 2 * p + 2)
+                    r2[w, both, rows] = r2[w, both, rows] + r1[w, 2 * p + z_lo, :, rows]
+                rs_start(u, 2, [(r2.at[w, pl.ds(2 * (1 - z_hi), 2), rows], r3.at[w, :, rows])], to_far)
+            else:
+                r2[w, :, rows] = r2[w, :, rows] + r1[w, :, ens, rows]
+                rs_start(u, 2, [(r2.at[w, 2 * p + 1 - z_lo, rows], r3.at[w, p, rows]) for p in range(2)], to_z)
+        elif stage == 3:
+            for p in range(2):
+                own = r2[w, 2 * z_hi + p, rows] if z_first else r2[w, 2 * p + z_lo, rows]
+                r3[w, p, rows] = r3[w, p, rows] + own
+            if z_first:
+                rs_start(u, 3, [(r3.at[w, 1 - ens, rows], r4.at[w, rows])], to_x)
+            else:
+                rs_start(u, 3, [(r3.at[w, 1 - z_hi, rows], r4.at[w, rows])], to_far)
+        else:
+            own = r3[w, ens, rows] if z_first else r3[w, z_hi, rows]
+            out_w[w, rows] = r4[w, rows] + own
 
     tile_g = ne_g // 4 if (ne_g // 4) % 16 == 0 else 128
     tile_m = tile_of(ne_m, 512)
@@ -322,8 +362,7 @@
     halo = exchange(1)
     put_table(0, dot3(mid_s, wt(PS)))
     put_table(tm, dot3(mid_s, wt(PR)))
-    arrived(halo)
-    halo_s = split(land[1].reshape(nh, d))
+    halo_s = split(halo_arrived(1, halo))
     put_table(nm, dot3(halo_s, wt(PS)))
     act_m = dtab
     gather(mcol_s, mcol_r, ne_m, tm, tile_m, act_m)
@@ -338,23 +377,29 @@
     send_buf[2] = dtab[nm:tm, :].reshape(bands, 16, d)
     halo = exchange(2)
     store_dw(P2, sum_m, d_agg_s)
-    rs1(P2)
+    rs(0, 0)
     d_recv_s = split(dot2(incidence(medge_in, ne_m), (eh[0:ne_m, :], el[0:ne_m, :])))
     store_dw(PR, mid_s, d_recv_s)
-    rs1(PR)
+    rs(1, 0)
+    rs(0, 1)
     both = [jnp.concatenate([a, b], axis=0) for a, b in zip(mid_s, halo_s)]
     store_dw(PS, both, split(dtab[0:tm, :]))
-    rs1(PS)
+    rs(2, 0)
+    rs(1, 1)
     d_mid = cot + dot3(d_recv_s, wt(PR), 1, 1)
-    rs2(P2)
-    arrived(halo)
-    own = dtab[0:nm, :] + dot2(pick_m[...], split(land[2].reshape(nh, d)), 0, 0)
+    own = dtab[0:nm, :] + dot2(pick_m[...], split(halo_arrived(2, halo)), 0, 0)
+    rs(2, 1)
     d_mid = d_mid + dot3(split(own), wt(PS), 1, 1)
 
     d_agg, d_gain_g = norm_back(d_mid, unit_g, rstd_g, gains_in[0:1, :])
     if fused:
-        row = lax.broadcasted_iota(jnp.int32, (8, d), 0)
-        gain_mine[...] = jnp.where(row == 0, d_gain_g, jnp.where(row == 1, d_gain_p, 0.0))
+        row = lax.broadcasted_iota(jnp.int32, (8, quarter), 0)
+        packed = jnp.zeros((8, quarter), F32)
+        for g, gain in enumerate((d_gain_g, d_gain_p)):
+            full = jnp.broadcast_to(gain, (8, d))
+            for c in range(4):
+                packed = jnp.where(row == 4 * g + c, full[:, c * quarter : (c + 1) * quarter], packed)
+        gain_mine[...] = packed
         gain_copies = []
         for o in range(1, n_all):
             c = pltpu.make_async_remote_copy(
@@ -368,22 +413,23 @@
         out_gain[1:2, :] = d_gain_p
     d_agg_s = split(d_agg)
     store_dw(G2, sum_g, d_agg_s)
-    rs1(G2)
-    rs2(PR)
-    rs2(PS)
+    rs(3, 0)
     back(col_r, ne_g, tile_g, act_d, split(dot3(d_agg_s, wt(G2), 1, 1)))
+    rs(0, 2)
+    rs(3, 1)
+    rs(1, 2)
     d_recv_s = split(dot2(incidence(gedge_in, ne_g), (eh[0:ne_g, :], el[0:ne_g, :])))
     store_dw(GR, mesh_s, d_recv_s)
-    rs1(GR)
-    rs2(G2)
-    rs3(P2)
+    rs(4, 0)
     scatter(gedge_in, ne_g, ng, nh, 128)
     send_buf[3] = dtab[ng:tg, :].reshape(bands, 16, d)
     halo = exchange(3)
-    rs2(GR)
-    rs3(PR)
-    scatter(gedge_in, ne_g, 0, ng, 256)
-    rs3(PS)
+    rs(4, 1)
+    rs(0, 3)
+    scatter(gedge_in, ne_g, 0, ng // 2, 256)
+    rs(2, 2)
+    rs(1, 3)
+    scatter(gedge_in, ne_g, ng // 2, ng // 2, 256)
 
     def split_dtab(r):
         hi, lo = split(dtab[pl.ds(r, 128), :])
@@ -394,35 +440,51 @@
     b = (eh[0:tg, :], el[0:tg, :])
     for t in range(4):
         cols = slice(t * 128, (t + 1) * 128)
-        dw[GS, t] = dot3((gh[0:tg, cols], gl[0:tg, cols]), b, 0, 0).reshape(dw.shape[2:])
-    rs1(GS)
-    rs3(G2)
+        put_dw(GS, t, dot3((gh[0:tg, cols], gl[0:tg, cols]), b, 0, 0))
+    rs(6, 0)
+    rs(5, 0)
+    rs(2, 3)
     out_mesh[0] = d_mid + dot3(d_recv_s, wt(GR), 1, 1)
-    arrived(halo)
-    ret = split(land[3].reshape(nh, d))
+    rs(6, 1)
+    rs(5, 1)
+    rs(3, 2)
+    ret = split(halo_arrived(3, halo))
 
     def grid_step(r):
         own = dtab[pl.ds(r, 256), :] + dot2(pick_g[:, pl.ds(r, 256)], ret, 0, 0)
         grid_v[pl.ds(r, 256), :] = dot3(split(own), wt(GS), 1, 1)
 
-    rs2(GS)
-    rs3(GR)
-    loop(ng, 256, grid_step)
+    loop(ng // 2, 256, grid_step)
+    rs(3, 3)
+    rs(4, 2)
+    loop(ng // 2, 256, lambda r: grid_step(r + ng // 2))
     out_copy = pltpu.make_async_copy(grid_v, out_grid.at[0], out_sem)
     out_copy.start()
-    rs3(GS)
-    for w in (P2, PR, PS, G2, GR, GS):
-        rs4(w)
+    for u in (0, 1, 2):
+        rs(u, 4)
+    rs(6, 2)
+    rs(4, 3)
+    rs(5, 2)
+    rs(6, 3)
+    rs(5, 3)
     if fused:
         arrived(gain_copies)
         total = gain_mine[...]
         for o in range(n_all - 1):
             total = total + gain_land[o]
         width = d // n_all
+        per = quarter // width
+        row = lax.broadcasted_iota(jnp.int32, (8, quarter), 0)
+        line = [
+            jnp.sum(jnp.where(row == 4 * g + flat // per, total, 0.0), axis=0, keepdims=True) for g in range(2)
+        ]
+        wide = jnp.where(row == 0, line[0], jnp.where(row == 1, line[1], 0.0))
         mine = jnp.zeros((8, width), F32)
-        for j in range(n_all):
-            mine = jnp.where(flat == j, total[:, j * width : (j + 1) * width], mine)
+        for j in range(per):
+            mine = jnp.where(lax.rem(flat, per) == j, wide[:, j * width : (j + 1) * width], mine)
         out_gain[...] = mine[0:2]
+    for u in (3, 4, 6, 5):
+        rs(u, 4)
     for c in sends:
         c.wait_send()
     out_copy.wait()
@@ -459,6 +521,8 @@
         pltpu.VMEM((nh, nm), BF16),
         pltpu.VMEM((4, bands, 16, d), F32),
         pltpu.VMEM((4, bands, 16, d), F32),
+        pltpu.VMEM((4, bands, 8, d // 4), F32),
+        pltpu.VMEM((4, bands, 8, d // 4), F32),
         pltpu.SemaphoreType.DMA((7,)),
         pltpu.SemaphoreType.DMA((4, bands)),
         pltpu.SemaphoreType.DMA((4, bands)),
@@ -466,18 +530,15 @@
     ]
     if fused:
         scratch += [
-            pltpu.VMEM((6, nz, nx, 2, rows, d), F32),
-            pltpu.VMEM((6, nz, nx, rows, d), F32),
-            pltpu.VMEM((6, nx - 1, nz, rows, d), F32),
-            pltpu.VMEM((6, nz - 1, rows, d), F32),
-            pltpu.VMEM((8, d), F32),
-            pltpu.VMEM((n_all - 1, 8, d), F32),
-            pltpu.SemaphoreType.DMA((6,)),
-            pltpu.SemaphoreType.DMA((6,)),
-            pltpu.SemaphoreType.DMA((6, nx - 1)),
-            pltpu.SemaphoreType.DMA((6, nx - 1)),
-            pltpu.SemaphoreType.DMA((6, nz - 1)),
-            pltpu.SemaphoreType.DMA((6, nz - 1)),
+            pltpu.VMEM((6, 2, 4, 2, rows, d), F32),
+            pltpu.VMEM((6, 4, 2, rows, d), F32),
+            pltpu.VMEM((6, 4, rows, d), F32),
+            pltpu.VMEM((6, 2, rows, d), F32),
+            pltpu.VMEM((6, rows, d), F32),
+            pltpu.VMEM((8, d // 4), F32),
+            pltpu.VMEM((n_all - 1, 8, d // 4), F32),
+            pltpu.SemaphoreType.DMA((len(UNITS), 4, 2)),
+            pltpu.SemaphoreType.DMA((len(UNITS), 4, 2)),
             pltpu.SemaphoreType.DMA((n_all - 1,)),
             pltpu.SemaphoreType.DMA((n_all - 1,)),
         ]
@@ -511,7 +572,7 @@
 def solution(mesh):
     nz, nx, nr = mesh.shape["dom"], mesh.shape["ens"], mesh.shape["rep"]
     rows = 512 // (nz * nx * nr)
-    cfg = dict(bands=nz * nr, nx=nx, nz=nz, fused=nz == 4 and nx > 1 and rows % 8 == 0)
+    cfg = dict(bands=nz * nr, nx=nx, nz=nz, fused=nz == 4 and nx == 2 and rows % 16 == 0)
     return jax.shard_map(
         functools.partial(body, cfg),
         mesh=mesh,

time: 88.9 us -> 88.1 us (level)
  no operation moved by 1% of the time
where the time goes in v2:
time: 88.1 us; the launch traced here: 87.9 us
  Pallas kernels  82.1 us (93%)
  local copies, waits for them, and re-layouts  5.16 us (6%)
    pallas_call x1, Pallas kernels, body(): pl.pallas_call(functools.partial(kernel, cfg), out_shape=(jax.ShapeDtypeS...  82.1 us
    unnamed x10, local copies, waits for them, and re-layouts  5.16 us

profile of v2, /device:TPU:0, one launch (start us, length us, event | category | flops | bytes accessed | tf_op | source)
XLA Modules:
  0.0 87.9 jit_solution(7683451310569071120)
XLA Ops:
  0.6 82.1 %shard_map.120 = (f32[1,1024,512]{2,1,0:T(8,128)}, f32[1,128,512]{2,1,0:T(8,128)}, f32[6,32,512]{2,1,0:T(8,128)}, f32[2,32]{1,0:T(2,128)}) custom-call(f32[1,1024,512]{2,1,0:T(8,128)} %grid_in.1, f32[1,128,512]{2,1,0:T(8,128)} %mesh_in.1, f32[1,128,512]{2,1,0:T(8,128)} %cot_in.1, f32[6,512,512]{2,1,0:T(8,128)} %w_in.1, f32[2,512]{1,0:T(2,128)} %gains_in.1, ...), custom_call_target="tpu_custom_call" | custom-call | tf_op jit(solution)/shard_map/pallas_call | solution.py:550
  82.8 0.0 copy-start.1
  82.8 0.0 copy-start
  82.8 0.0 copy-start.2
  82.8 3.1 %copy.17 = f32[1,1024,512]{2,1,0:T(8,128)} copy(f32[1,1024,512]{2,1,0:T(8,128)} %get-tuple-element.8) | data formatting | bytes 4194304
  85.9 0.0 copy-done.1
  85.9 0.7 copy.18
  86.6 0.0 copy-done
  86.6 0.7 copy.19
  87.4 0.0 copy-done.2
  87.4 0.6 copy.20
Async XLA Ops:
  82.8 3.2 %copy-start.1 = (f32[1,128,512]{2,1,0:T(8,128)S(1)}, f32[1,128,512]{2,1,0:T(8,128)}, u32[]{:S(2)}) copy-start(f32[1,128,512]{2,1,0:T(8,128)} %get-tuple-element.9) | copy-start | bytes 786436
  82.8 3.9 %copy-start = (f32[6,32,512]{2,1,0:T(8,128)S(1)}, f32[6,32,512]{2,1,0:T(8,128)}, u32[]{:S(2)}) copy-start(f32[6,32,512]{2,1,0:T(8,128)} %get-tuple-element.10) | copy-start | bytes 1179652
  82.8 4.6 %copy-start.2 = (f32[2,32]{1,0:T(2,128)S(1)}, f32[2,32]{1,0:T(2,128)}, u32[]{:S(2)}) copy-start(f32[2,32]{1,0:T(2,128)} %get-tuple-element.11) | copy-start | bytes 772
